TPU v7x, 32 devices: a whole 2x2x4 slice. The times are simulated.
32 devices in a mesh: samp: 8 (over y, x, core), var: 4 (over z).
Axes of the slice: x: 2, y: 2, z: 4, core: 2. Of those that a mesh axis runs over, the one named last changes fastest.
Arguments:
- genotypes: int32 [8192, 4096], P('samp', 'var'), may hold values from 0 to 2
- observed: int32 [8192, 4096], P('samp', 'var'), may hold values from 0 to 1, as said below
- proportions: float32 [10, 8192], P(None, 'samp'), may hold values from 0 to 1, as said below
- frequencies: float32 [10, 4096], P(None, ('samp', 'var')), may hold values from 0.02 to 0.98
Outputs:
- mixture: float32 [10, 8192], P(None, 'samp')
- alleles: float32 [10, 4096], P(None, 'var')
Inputs may be any that keep to these rules, and one draw needn't show every extreme that they name: Every sample is observed at 256 or more variants and every variant at 512 or more samples. Each sample's 10 proportions are positive and sum to one.
All inputs are finite; a program needn't handle non-finite values.
Results may differ from a plain program's by a relative error of at most 0.0003.
Values sent between devices are 32-bit elements; how exact they have to be, the bound alone decides.
No kernel may reach another device: no remote copies, remote signals or barrier semaphores. Data moves between devices by JAX's collectives and lax.ppermute only.
A program may use at most 128 MiB of HBM per device.

v0:
```python
import jax
import jax.numpy as jnp
from jax import lax
from jax.sharding import PartitionSpec as P

STEPS = 2


CLIP_LOW = 1e-05
NORM_EPS = 1e-10
EXACT = lax.Precision.HIGHEST


def clip_unit(values):
    return jnp.clip(values, CLIP_LOW, 1.0 - CLIP_LOW)


def tidy_mixture(mixture):
    clipped = clip_unit(mixture)
    return clipped / jnp.sum(clipped, axis=0, keepdims=True)


def step_size(first, second):
    return jnp.maximum(1.0, jnp.sqrt(first / (second + NORM_EPS)))


def allele_rule(alleles, alt_sums, ref_sums):
    weighted = alleles * alt_sums
    return clip_unit(weighted / (weighted + (1.0 - alleles) * ref_sums))


def local(genotypes, observed, proportions, frequencies):
    samp_count = lax.axis_size("samp")
    var_count = lax.axis_size("var")
    populations = frequencies.shape[0]
    block_width = frequencies.shape[1]
    by_sample = lax.all_gather(frequencies, "samp", axis=1, tiled=True)
    by_sample = by_sample.reshape(populations, var_count, samp_count // var_count, block_width)
    arrived = lax.all_to_all(by_sample, "var", split_axis=1, concat_axis=1, tiled=True)
    alleles = jnp.transpose(arrived, (0, 2, 1, 3)).reshape(populations, -1)
    seen_vals = observed.astype(jnp.float32)
    geno_vals = genotypes.astype(jnp.float32)
    alt_counts = seen_vals * geno_vals
    ref_counts = seen_vals * (2.0 - geno_vals)
    local_counts = jnp.sum(observed, axis=1).astype(jnp.float32)
    twice_observed = 2.0 * lax.psum(local_counts, "var")[None, :]

    def expectation_step(mixture, current):
        expected = lax.dot_general(
            mixture,
            current,
            (((0,), (0,)), ((), ())),
            precision=EXACT,
            preferred_element_type=jnp.float32,
        )
        ratio_alt = alt_counts / expected
        ratio_ref = ref_counts / (1.0 - expected)
        prop_terms = lax.dot_general(
            current,
            ratio_alt - ratio_ref,
            (((1,), (1,)), ((), ())),
            precision=EXACT,
            preferred_element_type=jnp.float32,
        )
        prop_terms = prop_terms + jnp.sum(ratio_ref, axis=1)[None, :]
        alt_terms = lax.dot_general(
            mixture,
            ratio_alt,
            (((1,), (0,)), ((), ())),
            precision=EXACT,
            preferred_element_type=jnp.float32,
        )
        ref_terms = lax.dot_general(
            mixture,
            ratio_ref,
            (((1,), (0,)), ((), ())),
            precision=EXACT,
            preferred_element_type=jnp.float32,
        )
        prop_sums = lax.psum(prop_terms, "var")
        next_mixture = clip_unit(mixture * prop_sums / twice_observed)
        alt_sums, ref_sums = lax.psum((alt_terms, ref_terms), "samp")
        next_alleles = allele_rule(current, alt_sums, ref_sums)
        return (next_mixture, next_alleles)

    mixture = proportions
    for repeat in range(STEPS):
        mixture_one, alleles_one = expectation_step(mixture, alleles)
        mixture_two, alleles_two = expectation_step(mixture_one, alleles_one)
        step_mix = mixture_one - mixture
        curve_mix = mixture_two - mixture_one - step_mix
        step_allele = alleles_one - alleles
        curve_allele = alleles_two - alleles_one - step_allele
        step_mix_local = jnp.sum(step_mix * step_mix)
        curve_mix_local = jnp.sum(curve_mix * curve_mix)
        step_allele_local = jnp.sum(step_allele * step_allele)
        curve_allele_local = jnp.sum(curve_allele * curve_allele)
        step_allele_sum, curve_allele_sum = lax.psum((step_allele_local, curve_allele_local), "var")
        step_mix_sum, curve_mix_sum = lax.psum((step_mix_local, curve_mix_local), "samp")
        alpha_mix = step_size(step_mix_sum, curve_mix_sum)
        alpha_allele = step_size(step_allele_sum, curve_allele_sum)
        extra_mix = tidy_mixture(
            mixture + 2.0 * alpha_mix * step_mix + alpha_mix * alpha_mix * curve_mix
        )
        extra_allele = clip_unit(
            alleles + 2.0 * alpha_allele * step_allele + alpha_allele * alpha_allele * curve_allele
        )
        mixture, alleles = expectation_step(extra_mix, extra_allele)
    return (mixture, alleles)


def solution(mesh):
    placed = (P("samp", "var"), P("samp", "var"), P(None, "samp"), P(None, ("samp", "var")))
    return jax.shard_map(
        local,
        mesh=mesh,
        in_specs=placed,
        out_specs=(P(None, "samp"), P(None, "var")),
        check_vma=False,
    )
```

profile of v0, /device:TPU:0, one launch (start us, length us, event | category | flops | bytes accessed | tf_op | source)
XLA Modules:
  0.0 582.9 jit_solution(17412179840368174260)
XLA Ops:
  7.2 10.7 %all_gather.3 = f32[10,1024]{1,0:T(8,128)S(1)} all-gather(f32[10,128]{1,0:T(8,128)} %param.7), channel_id=1, replica_groups=mesh['samp'=8,'var'=4] {'samp'}, dimensions={1}, use_global_device_ids=true | all-gather | bytes 46080 | tf_op jit(solution)/shard_map/all_gather | solution.py:37
  36.7 11.9 %fusion.73 = (f32[1024]{0:T(1024)S(1)}, f32[1024,1024]{0,1:T(8,128)S(1)}, f32[1024,1024]{0,1:T(8,128)}, f32[1024,1024]{0,1:T(8,128)S(1)}, f32[1024,1024]{0,1:T(8,128)S(1)}) fusion(s32[1024,1024]{0,1:T(8,128)} %copy.13, s32[1024,1024]{0,1:T(8,128)} %copy.12, f32[10,1024]{1,0:T(8,128)S(1)} %copy-done.11, f32[10,1024]{1,0:T(8,128)S(1)} %reshape.21), kind=kOutput, calls=%fused_computation.94 | convolution fusion | flops 134216704 | bytes 25251840 | tf_op jit(solution)/shard_map/dot_general | solution.py:49
  59.5 7.5 %fusion.15 = f32[10,1024]{1,0:T(8,128)S(1)} fusion(f32[10,1024]{1,0:T(8,128)S(1)} %reshape.21, f32[1024,1024]{0,1:T(8,128)} %copy-done, f32[1024]{0:T(1024)S(1)} %get-tuple-element.50, f32[1024,1024]{0,1:T(8,128)} %copy-done.4, f32[1024,1024]{0,1:T(8,128)} %copy-done.10), kind=kOutput, calls=%fused_computation.21 | convolution fusion | flops 127936512 | bytes 12668928 | tf_op jit(solution)/shard_map/dot_general | solution.py:58
  67.0 20.6 %all-reduce.8 = (f32[10,1024]{1,0:T(8,128)S(1)}, f32[1024]{0:T(1024)S(1)}) all-reduce(f32[10,1024]{1,0:T(8,128)S(1)} %fusion.15, f32[1024]{0:T(1024)S(1)} %convert_element_type.11), channel_id=1, replica_groups=mesh['samp'=8,'var'=4] {'var'}, use_global_device_ids=true, to_apply=%region_1.0 | all-reduce | flops 11264 | bytes 90112 | tf_op jit(solution)/shard_map/psum | solution.py:80
  87.7 50.3 %all-reduce.22.cloned.1.call-done = (f32[10,1024]{1,0:T(8,128)}, f32[10,1024]{1,0:T(8,128)}) async-done(((f32[10,1024]{1,0:T(8,128)}, f32[10,1024]{1,0:T(8,128)}), (f32[10,1024]{1,0:T(8,128)}, f32[10,1024]{1,0:T(8,128)})) %all-reduce.22.cloned.1.call-update) | async-done | bytes 81936 | tf_op jit(solution)/shard_map/psum | solution.py:82
  138.9 9.2 %fusion.72 = (f32[1024]{0:T(1024)S(1)}, f32[1024,1024]{0,1:T(8,128)S(1)}, f32[1024,1024]{0,1:T(8,128)S(1)}) fusion(f32[1024,1024]{0,1:T(8,128)} %get-tuple-element.52, f32[10,1024]{1,0:T(8,128)S(1)} %divide_clamp_fusion.3, f32[10,1024]{1,0:T(8,128)S(1)} %fusion.33), kind=kOutput, calls=%fused_computation.93 | convolution fusion | flops 128973824 | bytes 12668928 | tf_op jit(solution)/shard_map/dot_general | solution.py:49
  157.9 19.6 %psum.194 = f32[10,1024]{1,0:T(8,128)S(1)} all-reduce(f32[10,1024]{1,0:T(8,128)S(1)} %fusion.18), channel_id=1, replica_groups=mesh['samp'=8,'var'=4] {'var'}, use_global_device_ids=true, to_apply=%region_9.10 | all-reduce | flops 10240 | bytes 81920 | tf_op jit(solution)/shard_map/psum | solution.py:80
  178.1 24.0 %all-reduce.23 = (f32[10,1024]{1,0:T(8,128)S(1)}, f32[10,1024]{1,0:T(8,128)S(1)}, f32[]{:T(128)}, f32[]{:T(128)}) all-reduce(f32[10,1024]{1,0:T(8,128)S(1)} %fusion.74, f32[10,1024]{1,0:T(8,128)S(1)} %fusion.59, f32[]{:T(128)} %get-tuple-element.5, f32[]{:T(128)} %get-tuple-element.4), channel_id=1, replica_groups=mesh['samp'=8,'var'=4] {'samp'}, use_global_device_ids=true, to_apply=%region_16.17 | all-reduce | flops 20482 | bytes 163856 | tf_op jit(solution)/shard_map/psum | solution.py:82
  204.7 9.4 %all-reduce.7 = (f32[]{:T(128)}, f32[]{:T(128)}) all-reduce(f32[]{:T(128)} %multiply_reduce_fusion.5, f32[]{:T(128)} %get-tuple-element.44), channel_id=1, replica_groups=mesh['samp'=8,'var'=4] {'var'}, use_global_device_ids=true, to_apply=%region_14.15 | all-reduce | flops 2 | bytes 16 | tf_op jit(solution)/shard_map/psum | solution.py:98
  215.5 9.0 %fusion.69 = (f32[1024]{0:T(1024)S(1)}, f32[1024,1024]{0,1:T(8,128)S(1)}, f32[1024,1024]{0,1:T(8,128)S(1)}) fusion(f32[1024,1024]{0,1:T(8,128)} %get-tuple-element.52, f32[10,1024]{1,0:T(8,128)S(1)} %get-tuple-element.60, f32[10,1024]{1,0:T(8,128)S(1)} %get-tuple-element.43, f32[1024]{0:T(1024)S(1)} %get-tuple-element.42), kind=kOutput, calls=%fused_computation.91 | convolution fusion | flops 128984064 | bytes 12673024 | tf_op jit(solution)/shard_map/dot_general | solution.py:49
  233.0 7.3 %fusion.21 = f32[10,1024]{1,0:T(8,128)S(1)} fusion(f32[10,1024]{1,0:T(8,128)S(1)} %get-tuple-element.60, f32[1024,1024]{0,1:T(8,128)} %copy-done.2, f32[1024]{0:T(1024)S(1)} %get-tuple-element.40, f32[1024,1024]{0,1:T(8,128)} %copy-done.4, f32[1024,1024]{0,1:T(8,128)} %copy-done.13), kind=kOutput, calls=%fused_computation.23 | convolution fusion | flops 127936512 | bytes 12668928 | tf_op jit(solution)/shard_map/dot_general | solution.py:58
  240.3 18.3 %psum.200 = f32[10,1024]{1,0:T(8,128)S(1)} all-reduce(f32[10,1024]{1,0:T(8,128)S(1)} %fusion.21), channel_id=1, replica_groups=mesh['samp'=8,'var'=4] {'var'}, use_global_device_ids=true, to_apply=%region_20.21 | all-reduce | flops 10240 | bytes 81920 | tf_op jit(solution)/shard_map/psum | solution.py:80
  258.7 49.9 %all-reduce.20.cloned.1.call-done = (f32[10,1024]{1,0:T(8,128)}, f32[10,1024]{1,0:T(8,128)}) async-done(((f32[10,1024]{1,0:T(8,128)}, f32[10,1024]{1,0:T(8,128)}), (f32[10,1024]{1,0:T(8,128)}, f32[10,1024]{1,0:T(8,128)})) %all-reduce.20.cloned.1.call-update) | async-done | bytes 81936 | tf_op jit(solution)/shard_map/psum | solution.py:82
  309.5 9.2 %fusion.68 = (f32[1024]{0:T(1024)S(1)}, f32[1024,1024]{0,1:T(8,128)S(1)}, f32[1024,1024]{0,1:T(8,128)S(1)}) fusion(f32[1024,1024]{0,1:T(8,128)} %get-tuple-element.52, f32[10,1024]{1,0:T(8,128)S(1)} %divide_clamp_fusion.2, f32[10,1024]{1,0:T(8,128)S(1)} %fusion.37), kind=kOutput, calls=%fused_computation.90 | convolution fusion | flops 128973824 | bytes 12668928 | tf_op jit(solution)/shard_map/dot_general | solution.py:49
  327.1 7.3 %fusion.24 = f32[10,1024]{1,0:T(8,128)S(1)} fusion(f32[10,1024]{1,0:T(8,128)S(1)} %fusion.37, f32[1024,1024]{0,1:T(8,128)} %copy-done.3, f32[1024]{0:T(1024)S(1)} %get-tuple-element.38, f32[1024,1024]{0,1:T(8,128)} %copy-done.4, f32[1024,1024]{0,1:T(8,128)} %copy-done.14), kind=kOutput, calls=%fused_computation.24 | convolution fusion | flops 127936512 | bytes 12668928 | tf_op jit(solution)/shard_map/dot_general | solution.py:58
  334.4 19.6 %psum.203 = f32[10,1024]{1,0:T(8,128)S(1)} all-reduce(f32[10,1024]{1,0:T(8,128)S(1)} %fusion.24), channel_id=1, replica_groups=mesh['samp'=8,'var'=4] {'var'}, use_global_device_ids=true, to_apply=%region_24.25 | all-reduce | flops 10240 | bytes 81920 | tf_op jit(solution)/shard_map/psum | solution.py:80
  354.2 49.8 %all-reduce.18.cloned.1.call-done = (f32[10,1024]{1,0:T(8,128)}, f32[10,1024]{1,0:T(8,128)}) async-done(((f32[10,1024]{1,0:T(8,128)}, f32[10,1024]{1,0:T(8,128)}), (f32[10,1024]{1,0:T(8,128)}, f32[10,1024]{1,0:T(8,128)})) %all-reduce.18.cloned.1.call-update) | async-done | bytes 81936 | tf_op jit(solution)/shard_map/psum | solution.py:82
  404.9 9.2 %fusion.67 = (f32[1024]{0:T(1024)S(1)}, f32[1024,1024]{0,1:T(8,128)S(1)}, f32[1024,1024]{0,1:T(8,128)S(1)}) fusion(f32[1024,1024]{0,1:T(8,128)} %get-tuple-element.52, f32[10,1024]{1,0:T(8,128)S(1)} %divide_clamp_fusion.1, f32[10,1024]{1,0:T(8,128)S(1)} %fusion.38), kind=kOutput, calls=%fused_computation.89 | convolution fusion | flops 128973824 | bytes 12668928 | tf_op jit(solution)/shard_map/dot_general | solution.py:49
  423.8 19.6 %psum.207 = f32[10,1024]{1,0:T(8,128)S(1)} all-reduce(f32[10,1024]{1,0:T(8,128)S(1)} %fusion.27), channel_id=1, replica_groups=mesh['samp'=8,'var'=4] {'var'}, use_global_device_ids=true, to_apply=%region_30.31 | all-reduce | flops 10240 | bytes 81920 | tf_op jit(solution)/shard_map/psum | solution.py:80
  444.1 24.0 %all-reduce.24 = (f32[10,1024]{1,0:T(8,128)S(1)}, f32[10,1024]{1,0:T(8,128)S(1)}, f32[]{:T(128)}, f32[]{:T(128)}) all-reduce(f32[10,1024]{1,0:T(8,128)S(1)} %fusion.76, f32[10,1024]{1,0:T(8,128)S(1)} %fusion.51, f32[]{:T(128)} %get-tuple-element.3, f32[]{:T(128)} %get-tuple-element.2), channel_id=1, replica_groups=mesh['samp'=8,'var'=4] {'samp'}, use_global_device_ids=true, to_apply=%region_37.38 | all-reduce | flops 20482 | bytes 163856 | tf_op jit(solution)/shard_map/psum | solution.py:82
  470.7 9.2 %all-reduce.6 = (f32[]{:T(128)}, f32[]{:T(128)}) all-reduce(f32[]{:T(128)} %multiply_reduce_fusion.1, f32[]{:T(128)} %get-tuple-element.32), channel_id=1, replica_groups=mesh['samp'=8,'var'=4] {'var'}, use_global_device_ids=true, to_apply=%region_35.36 | all-reduce | flops 2 | bytes 16 | tf_op jit(solution)/shard_map/psum | solution.py:98
  481.3 9.0 %fusion.64 = (f32[1024]{0:T(1024)S(1)}, f32[1024,1024]{0,1:T(8,128)S(1)}, f32[1024,1024]{0,1:T(8,128)S(1)}) fusion(f32[1024,1024]{0,1:T(8,128)} %get-tuple-element.52, f32[10,1024]{1,0:T(8,128)S(1)} %add_clamp_fusion, f32[10,1024]{1,0:T(8,128)S(1)} %get-tuple-element.31, f32[1024]{0:T(1024)S(1)} %get-tuple-element.30), kind=kOutput, calls=%fused_computation.87 | convolution fusion | flops 128984064 | bytes 12673024 | tf_op jit(solution)/shard_map/dot_general | solution.py:49
  506.1 18.3 %psum.213 = f32[10,1024]{1,0:T(8,128)S(1)} all-reduce(f32[10,1024]{1,0:T(8,128)S(1)} %fusion.30), channel_id=1, replica_groups=mesh['samp'=8,'var'=4] {'var'}, use_global_device_ids=true, to_apply=%region_41.42 | all-reduce | flops 10240 | bytes 81920 | tf_op jit(solution)/shard_map/psum | solution.py:80
  525.1 49.3 %all-reduce.16.cloned.1.call-done = (f32[10,1024]{1,0:T(8,128)}, f32[10,1024]{1,0:T(8,128)}) async-done(((f32[10,1024]{1,0:T(8,128)}, f32[10,1024]{1,0:T(8,128)}), (f32[10,1024]{1,0:T(8,128)}, f32[10,1024]{1,0:T(8,128)})) %all-reduce.16.cloned.1.call-update) | async-done | bytes 81936 | tf_op jit(solution)/shard_map/psum | solution.py:82
  (81 shorter events, 90.7 us)
Async XLA Ops:
  18.5 18.1 %all-to-all-start = ((f32[10,4,2,128]{3,2,0,1:T(2,128)}), f32[10,4,2,128]{3,2,0,1:T(2,128)S(1)}, u32[]{:S(2)}, u32[]{:S(2)}) async-start(f32[10,4,2,128]{3,2,0,1:T(2,128)} %copy.14), calls=%async_computation | async-start | bytes 81920 | tf_op jit(solution)/shard_map/all_to_all | solution.py:39
  23.4 114.6 %all-reduce.22.cloned.1.call-start = ((), (), s32[]{:S(2)}) async-start(), calls=%async_computation.4 | async-start | bytes 262144 | tf_op jit(solution)/shard_map/psum | solution.py:82
  31.2 5.5 copy-start.11
  48.6 2.0 copy-start
  48.6 6.2 %copy-start.4 = (f32[1024,1024]{0,1:T(8,128)}, f32[1024,1024]{0,1:T(8,128)S(1)}, u32[]{:S(2)}) copy-start(f32[1024,1024]{0,1:T(8,128)S(1)} %get-tuple-element.53) | copy-start | bytes 12582916
  48.6 6.2 %copy-start.10 = (f32[1024,1024]{0,1:T(8,128)}, f32[1024,1024]{0,1:T(8,128)S(1)}, u32[]{:S(2)}) copy-start(f32[1024,1024]{0,1:T(8,128)S(1)} %get-tuple-element.54) | copy-start | bytes 12582916
  87.6 221.0 %all-reduce.20.cloned.1.call-start = ((), (), s32[]{:S(2)}) async-start(), calls=%async_computation.3 | async-start | bytes 262144 | tf_op jit(solution)/shard_map/psum | solution.py:82
  138.9 9.2 %copy-start.5 = (f32[1024,1024]{0,1:T(8,128)S(1)}, f32[1024,1024]{0,1:T(8,128)}, u32[]{:S(2)}) copy-start(f32[1024,1024]{0,1:T(8,128)} %copy-done.4) | copy-start | bytes 12582916
  215.5 9.1 %copy-start.6 = (f32[1024,1024]{0,1:T(8,128)S(1)}, f32[1024,1024]{0,1:T(8,128)}, u32[]{:S(2)}) copy-start(f32[1024,1024]{0,1:T(8,128)} %copy-done.4) | copy-start | bytes 12582916
  224.5 4.2 copy-start.13
  224.5 4.2 copy-start.2
  258.6 145.4 %all-reduce.18.cloned.1.call-start = ((), (), s32[]{:S(2)}) async-start(), calls=%async_computation.2 | async-start | bytes 262144 | tf_op jit(solution)/shard_map/psum | solution.py:82
  309.5 9.2 %copy-start.7 = (f32[1024,1024]{0,1:T(8,128)S(1)}, f32[1024,1024]{0,1:T(8,128)}, u32[]{:S(2)}) copy-start(f32[1024,1024]{0,1:T(8,128)} %copy-done.4) | copy-start | bytes 12582916
  318.7 4.2 copy-start.14
  318.7 4.2 copy-start.3
  354.1 220.3 %all-reduce.16.cloned.1.call-start = ((), (), s32[]{:S(2)}) async-start(), calls=%async_computation.1 | async-start | bytes 262144 | tf_op jit(solution)/shard_map/psum | solution.py:82
  404.8 9.2 %copy-start.8 = (f32[1024,1024]{0,1:T(8,128)S(1)}, f32[1024,1024]{0,1:T(8,128)}, u32[]{:S(2)}) copy-start(f32[1024,1024]{0,1:T(8,128)} %copy-done.4) | copy-start | bytes 12582916
  481.3 9.1 %copy-start.9 = (f32[1024,1024]{0,1:T(8,128)S(1)}, f32[1024,1024]{0,1:T(8,128)}, u32[]{:S(2)}) copy-start(f32[1024,1024]{0,1:T(8,128)} %copy-done.4) | copy-start | bytes 12582916
  490.4 4.2 copy-start.12
  490.4 4.2 copy-start.1
Sparse Core Ops, SparseCore 0:
  87.7 50.1 all-reduce.21
  258.7 49.8 all-reduce.19
  354.2 49.7 all-reduce.17
  524.5 49.8 all-reduce.15
where the time goes:
time: 588 us; the launch traced here: 583 us
  waiting for transfers between devices  199 us (34%)
  blocking collectives  193 us (33%)
  matrix products  141 us (24%)
  between operations  19.9 us (3%)
  local copies, waits for them, and re-layouts  13.5 us (2%)
  other arithmetic  11.3 us (2%)
    psum x4, waiting for transfers between devices, expectation_step(): alt_sums, ref_sums = lax.psum((alt_terms, ref_terms), 'samp')  199 us
    psum x6, blocking collectives, expectation_step(): prop_sums = lax.psum(prop_terms, 'var')  116 us
    dot_general x6, matrix products, expectation_step(): lax.dot_general(mixture, current, (((0,), (0,)), ((), ())), precision=EXA...  57.6 us
    psum x2, blocking collectives, expectation_step(): alt_sums, ref_sums = lax.psum((alt_terms, ref_terms), 'samp')  47.9 us
    dot_general x6, matrix products, expectation_step(): lax.dot_general(current, ratio_alt - ratio_ref, (((1,), (1,)), ((), ())),...  34.8 us
    dot_general x6, matrix products, expectation_step(): lax.dot_general(mixture, ratio_alt, (((1,), (0,)), ((), ())), precision=E...  24.2 us
    dot_general x6, matrix products, expectation_step(): lax.dot_general(mixture, ratio_ref, (((1,), (0,)), ((), ())), precision=E...  24 us
    psum x2, blocking collectives, local(): lax.psum((step_allele_local, curve_allele_local), 'var')  18.6 us
  transfers between devices with their start and end apart: 5, of which 4 were waited for; matrix products, arithmetic and copies ran while one was open for 2% of the time, Pallas kernels for 0%

commit v1 on v0

--- a/solution.py
+++ b/solution.py
@@ -29,6 +29,34 @@
     return clip_unit(weighted / (weighted + (1.0 - alleles) * ref_sums))
 
 
+def exchange_sums(axis, first_radix):
+    size = lax.axis_size(axis)
+    rounds = []
+    stride = 1
+    while stride < size:
+        left = size // stride
+        radix = first_radix if stride == 1 and left % first_radix == 0 else 4
+        while left % radix:
+            radix //= 2
+        if radix < 2:
+            return lambda value: lax.psum(value, axis)
+        rounds.append((stride, radix))
+        stride *= radix
+
+    def swap(value, mask):
+        return lax.ppermute(value, axis, [(i, i ^ mask) for i in range(size)])
+
+    def total(value):
+        for stride, radix in rounds:
+            parts = [value] + [swap(value, stride * m) for m in range(1, radix)]
+            while len(parts) > 1:
+                parts = [a + b for a, b in zip(parts[::2], parts[1::2])]
+            value = parts[0]
+        return value
+
+    return total
+
+
 def local(genotypes, observed, proportions, frequencies):
     samp_count = lax.axis_size("samp")
     var_count = lax.axis_size("var")
@@ -42,10 +70,11 @@
     geno_vals = genotypes.astype(jnp.float32)
     alt_counts = seen_vals * geno_vals
     ref_counts = seen_vals * (2.0 - geno_vals)
-    local_counts = jnp.sum(observed, axis=1).astype(jnp.float32)
-    twice_observed = 2.0 * lax.psum(local_counts, "var")[None, :]
+    local_counts = jnp.sum(observed, axis=1).astype(jnp.float32)[None, :]
+    over_samp = exchange_sums("samp", 2)
+    over_var = exchange_sums("var", 4)
 
-    def expectation_step(mixture, current):
+    def expectation_sums(mixture, current):
         expected = lax.dot_general(
             mixture,
             current,
@@ -77,35 +106,51 @@
             precision=EXACT,
             preferred_element_type=jnp.float32,
         )
-        prop_sums = lax.psum(prop_terms, "var")
+        both_sums = over_samp(jnp.concatenate([alt_terms, ref_terms], axis=0))
+        return prop_terms, both_sums
+
+    def update(mixture, current, twice_observed, prop_sums, both_sums):
         next_mixture = clip_unit(mixture * prop_sums / twice_observed)
-        alt_sums, ref_sums = lax.psum((alt_terms, ref_terms), "samp")
-        next_alleles = allele_rule(current, alt_sums, ref_sums)
+        next_alleles = allele_rule(current, both_sums[:populations], both_sums[populations:])
         return (next_mixture, next_alleles)
 
     mixture = proportions
+    twice_observed = None
     for repeat in range(STEPS):
-        mixture_one, alleles_one = expectation_step(mixture, alleles)
-        mixture_two, alleles_two = expectation_step(mixture_one, alleles_one)
+        prop_terms, both_sums = expectation_sums(mixture, alleles)
+        if twice_observed is None:
+            joined = over_var(jnp.concatenate([prop_terms, local_counts], axis=0))
+            prop_sums = joined[:populations]
+            twice_observed = 2.0 * joined[populations:]
+        else:
+            prop_sums = over_var(prop_terms)
+        mixture_one, alleles_one = update(mixture, alleles, twice_observed, prop_sums, both_sums)
+        prop_terms, both_sums = expectation_sums(mixture_one, alleles_one)
+        mixture_two, alleles_two = update(
+            mixture_one, alleles_one, twice_observed, over_var(prop_terms), both_sums
+        )
         step_mix = mixture_one - mixture
         curve_mix = mixture_two - mixture_one - step_mix
         step_allele = alleles_one - alleles
         curve_allele = alleles_two - alleles_one - step_allele
-        step_mix_local = jnp.sum(step_mix * step_mix)
-        curve_mix_local = jnp.sum(curve_mix * curve_mix)
-        step_allele_local = jnp.sum(step_allele * step_allele)
-        curve_allele_local = jnp.sum(curve_allele * curve_allele)
-        step_allele_sum, curve_allele_sum = lax.psum((step_allele_local, curve_allele_local), "var")
-        step_mix_sum, curve_mix_sum = lax.psum((step_mix_local, curve_mix_local), "samp")
-        alpha_mix = step_size(step_mix_sum, curve_mix_sum)
-        alpha_allele = step_size(step_allele_sum, curve_allele_sum)
+        allele_squares = over_var(
+            jnp.stack([jnp.sum(step_allele * step_allele), jnp.sum(curve_allele * curve_allele)])
+        )
+        mix_squares = over_samp(
+            jnp.stack([jnp.sum(step_mix * step_mix), jnp.sum(curve_mix * curve_mix)])
+        )
+        alpha_mix = step_size(mix_squares[0], mix_squares[1])
+        alpha_allele = step_size(allele_squares[0], allele_squares[1])
         extra_mix = tidy_mixture(
             mixture + 2.0 * alpha_mix * step_mix + alpha_mix * alpha_mix * curve_mix
         )
         extra_allele = clip_unit(
             alleles + 2.0 * alpha_allele * step_allele + alpha_allele * alpha_allele * curve_allele
         )
-        mixture, alleles = expectation_step(extra_mix, extra_allele)
+        prop_terms, both_sums = expectation_sums(extra_mix, extra_allele)
+        mixture, alleles = update(
+            extra_mix, extra_allele, twice_observed, over_var(prop_terms), both_sums
+        )
     return (mixture, alleles)
 
 

time: 588 us -> 260 us (0.44)
  blocking collectives: 193 us -> 10.7 us
  waiting for transfers between devices: 199 us -> 44.6 us
  starting transfers between devices: 5 us -> 67.1 us
  matrix products: 141 us -> 91.1 us
  between operations: 19.9 us -> 6.64 us
  other arithmetic: 11.3 us -> 21.1 us
    psum x4 -> x0, waiting for transfers between devices: 199 us -> none  [expectation_step(): alt_sums, ref_sums = lax.psum((alt_terms, ref_terms), 'samp')]
    psum x10 -> x0, blocking collectives: 183 us -> none  [the longest x6 116 us: expectation_step(): prop_sums = lax.psum(prop_terms, 'var')]
    ppermute x0 -> x56, starting transfers between devices: none -> 62.2 us  [swap(): return lax.ppermute(value, axis, [(i, i ^ mask) for i in range(size)])]
    dot_general x24, matrix products: 141 us -> 91.1 us  [the longest x6 31.3 us: expectation_sums(): lax.dot_general(mixture, current, (((0,), (0,)), ((), ())), precision=EXA...]
    ppermute x0 -> x56, waiting for transfers between devices: none -> 44.6 us  [swap(): return lax.ppermute(value, axis, [(i, i ^ mask) for i in range(size)])]
    unnamed x32 -> x4, local copies, waits for them, and re-layouts: 12.8 us -> 10.8 us
  transfers between devices with their start and end apart: 5 -> 57, of which waited for: 4 -> 38; matrix products, arithmetic and copies ran while one was open for 2% -> 13% of each run, Pallas kernels for 0% -> 0%
where the time goes in v1:
time: 260 us; the launch traced here: 255 us
  matrix products  91.1 us (35%)
  starting transfers between devices  67.1 us (26%)
  waiting for transfers between devices  44.6 us (17%)
  other arithmetic  21.1 us (8%)
  local copies, waits for them, and re-layouts  13.9 us (5%)
  blocking collectives  10.7 us (4%)
  between operations  6.64 us (3%)
    ppermute x56, starting transfers between devices, swap(): return lax.ppermute(value, axis, [(i, i ^ mask) for i in range(size)])  62.2 us
    ppermute x56, waiting for transfers between devices, swap(): return lax.ppermute(value, axis, [(i, i ^ mask) for i in range(size)])  44.6 us
    dot_general x6, matrix products, expectation_sums(): lax.dot_general(mixture, current, (((0,), (0,)), ((), ())), precision=EXA...  31.3 us
    dot_general x6, matrix products, expectation_sums(): lax.dot_general(mixture, ratio_alt, (((1,), (0,)), ((), ())), precision=E...  21.8 us
    dot_general x6, matrix products, expectation_sums(): lax.dot_general(mixture, ratio_ref, (((1,), (0,)), ((), ())), precision=E...  21.3 us
    dot_general x6, matrix products, expectation_sums(): lax.dot_general(current, ratio_alt - ratio_ref, (((1,), (1,)), ((), ())),...  16.8 us
    unnamed x4, local copies, waits for them, and re-layouts  10.8 us
    all_gather x1, blocking collectives, local(): by_sample = lax.all_gather(frequencies, 'samp', axis=1, tiled=True)  10.7 us
  transfers between devices with their start and end apart: 57, of which 38 were waited for; matrix products, arithmetic and copies ran while one was open for 13% of the time, Pallas kernels for 0%

profile of v1, /device:TPU:0, one launch (start us, length us, event | category | flops | bytes accessed | tf_op | source)
XLA Modules:
  0.0 255.1 jit_solution(16568755819539609858)
XLA Ops:
  0.6 10.7 %all_gather.3 = f32[10,1024]{1,0:T(8,128)S(1)} all-gather(f32[10,128]{1,0:T(8,128)} %param.7), channel_id=1, replica_groups=mesh['samp'=8,'var'=4] {'samp'}, dimensions={1}, use_global_device_ids=true | all-gather | bytes 46080 | tf_op jit(solution)/shard_map/all_gather | solution.py:65
  12.0 4.9 %all-to-all-start = ((f32[10,4,2,128]{3,2,0,1:T(2,128)}), f32[10,4,2,128]{3,2,0,1:T(2,128)S(1)}, u32[]{:S(2)}, u32[]{:S(2)}) async-start(f32[10,4,2,128]{3,2,0,1:T(2,128)} %copy.14), calls=%async_computation | async-start | bytes 81920 | tf_op jit(solution)/shard_map/all_to_all | solution.py:67
  16.9 5.5 %copy.12 = s32[1024,1024]{0,1:T(8,128)} copy(s32[1024,1024]{1,0:T(8,128)} %param.5) | data formatting | bytes 8388608 | tf_op args[1]
  24.8 5.4 %copy.13 = s32[1024,1024]{0,1:T(8,128)} copy(s32[1024,1024]{1,0:T(8,128)} %param.4) | data formatting | bytes 8388608 | tf_op args[0]
  30.2 10.7 %fusion.78 = (f32[1024]{0:T(1024)S(1)}, f32[1024,1024]{0,1:T(8,128)S(1)}, f32[1024,1024]{0,1:T(8,128)S(1)}, f32[1024,1024]{0,1:T(8,128)S(1)}, f32[1024,1024]{0,1:T(8,128)S(1)}) fusion(s32[1024,1024]{0,1:T(8,128)} %copy.13, s32[1024,1024]{0,1:T(8,128)} %copy.12, f32[10,1024]{1,0:T(8,128)S(1)} %copy-done, f32[10,1024]{1,0:T(8,128)S(1)} %reshape.51), kind=kOutput, calls=%fused_computation.130 | convolution fusion | flops 134216704 | bytes 25251840 | tf_op jit(solution)/shard_map/dot_general | solution.py:78
  40.9 3.6 %convolution_bitcast_fusion = f32[10,1024]{1,0:T(8,128)S(1)} fusion(f32[1024,1024]{0,1:T(8,128)S(1)} %get-tuple-element.37, f32[10,1024]{1,0:T(8,128)S(1)} %copy-done), kind=kOutput, calls=%fused_computation.27 | convolution fusion | flops 125829120 | bytes 4276224 | tf_op jit(solution)/shard_map/dot_general | solution.py:102
  44.5 4.0 %convolution_bitcast_fusion.1 = f32[10,1024]{1,0:T(8,128)S(1)} fusion(f32[10,1024]{1,0:T(8,128)S(1)} %copy-done, f32[1024,1024]{0,1:T(8,128)S(1)} %get-tuple-element.39, f32[1024,1024]{0,1:T(8,128)S(1)} %get-tuple-element.48), kind=kOutput, calls=%fused_computation.28 | convolution fusion | flops 126877696 | bytes 8470528 | tf_op jit(solution)/shard_map/dot_general | solution.py:95
  51.4 3.0 %collective-permute-start.1 = (f32[11,1024]{1,0:T(8,128)S(1)}, f32[11,1024]{1,0:T(8,128)S(1)}, u32[]{:S(2)}, u32[]{:S(2)}) collective-permute-start(f32[11,1024]{1,0:T(8,128)S(1)} %pad_maximum_fusion.6), channel_id=1, source_target_pairs={{0,2},{1,3},{2,0},{3,1},{4,6},{5,7},{6,4},{7,5},{8,10},{9,11},{10,... | collective-permute-start | bytes 135176 | tf_op jit(solution)/shard_map/ppermute | solution.py:47
  57.3 3.3 %collective-permute-done.2 = f32[11,1024]{1,0:T(8,128)S(1)} collective-permute-done((f32[11,1024]{1,0:T(8,128)S(1)}, f32[11,1024]{1,0:T(8,128)S(1)}, u32[]{:S(2)}, u32[]{:S(2)}) %collective-permute-start.2) | collective-permute-done | bytes 45088 | tf_op jit(solution)/shard_map/ppermute | solution.py:47
  69.0 4.2 %fusion.75 = (f32[1024]{0:T(1024)S(1)}, f32[1024,1024]{0,1:T(8,128)S(1)}, f32[1024,1024]{0,1:T(8,128)S(1)}) fusion(f32[1024,1024]{0,1:T(8,128)S(1)} %get-tuple-element.38, f32[10,1024]{1,0:T(8,128)S(1)} %get-tuple-element.26, f32[10,1024]{1,0:T(8,128)S(1)} %get-tuple-element.33), kind=kOutput, calls=%fused_computation.129 | convolution fusion | flops 128973824 | bytes 12668928 | tf_op jit(solution)/shard_map/dot_general | solution.py:78
  73.2 3.5 %fusion.61 = f32[10,1024]{1,0:T(8,128)S(1)} fusion(f32[10,1024]{1,0:T(8,128)S(1)} %get-tuple-element.26, f32[1024,1024]{0,1:T(8,128)S(1)} %get-tuple-element.39, f32[1024,1024]{0,1:T(8,128)S(1)} %get-tuple-element.49), kind=kOutput, calls=%fused_computation.118 | convolution fusion | flops 126877696 | bytes 8470528 | tf_op jit(solution)/shard_map/dot_general | solution.py:95
  76.7 3.5 %fusion.83 = f32[10,1024]{1,0:T(8,128)S(1)} fusion(f32[10,1024]{1,0:T(8,128)S(1)} %get-tuple-element.26, f32[1024,1024]{0,1:T(8,128)S(1)} %get-tuple-element.30), kind=kOutput, calls=%fused_computation.135 | convolution fusion | flops 125829120 | bytes 4276224 | tf_op jit(solution)/shard_map/dot_general | solution.py:102
  121.7 4.4 %fusion.72 = (f32[1024]{0:T(1024)S(1)}, f32[1024,1024]{0,1:T(8,128)S(1)}, f32[1024,1024]{0,1:T(8,128)S(1)}) fusion(f32[1024,1024]{0,1:T(8,128)S(1)} %get-tuple-element.38, f32[10,1024]{1,0:T(8,128)S(1)} %get-tuple-element.54, f32[10,1024]{1,0:T(8,128)S(1)} %get-tuple-element.23, f32[1024]{0:T(1024)S(1)} %get-tuple-element.22), kind=kOutput, calls=%fused_computation.127 | convolution fusion | flops 128984064 | bytes 12673024 | tf_op jit(solution)/shard_map/dot_general | solution.py:78
  126.1 3.5 %fusion.46 = f32[10,1024]{1,0:T(8,128)S(1)} fusion(f32[10,1024]{1,0:T(8,128)S(1)} %get-tuple-element.23, f32[1024]{0:T(1024)S(1)} %get-tuple-element.22, f32[1024,1024]{0,1:T(8,128)S(1)} %get-tuple-element.39, f32[1024,1024]{0,1:T(8,128)S(1)} %get-tuple-element.50), kind=kOutput, calls=%fused_computation.103 | convolution fusion | flops 126887936 | bytes 8474624 | tf_op jit(solution)/shard_map/dot_general | solution.py:95
  129.6 3.5 %fusion.45 = f32[10,1024]{1,0:T(8,128)S(1)} fusion(f32[1024,1024]{0,1:T(8,128)S(1)} %get-tuple-element.21, f32[10,1024]{1,0:T(8,128)S(1)} %get-tuple-element.23, f32[1024]{0:T(1024)S(1)} %get-tuple-element.22), kind=kOutput, calls=%fused_computation.102 | convolution fusion | flops 125839360 | bytes 4280320 | tf_op jit(solution)/shard_map/dot_general | solution.py:102
  147.9 4.1 %fusion.71 = (f32[1024]{0:T(1024)S(1)}, f32[1024,1024]{0,1:T(8,128)S(1)}, f32[1024,1024]{0,1:T(8,128)S(1)}) fusion(f32[1024,1024]{0,1:T(8,128)S(1)} %get-tuple-element.38, f32[10,1024]{1,0:T(8,128)S(1)} %divide_clamp_fusion.2, f32[10,1024]{1,0:T(8,128)S(1)} %fusion.37), kind=kOutput, calls=%fused_computation.126 | convolution fusion | flops 128973824 | bytes 12668928 | tf_op jit(solution)/shard_map/dot_general | solution.py:78
  152.1 3.5 %fusion.56 = f32[10,1024]{1,0:T(8,128)S(1)} fusion(f32[10,1024]{1,0:T(8,128)S(1)} %divide_clamp_fusion.2, f32[1024,1024]{0,1:T(8,128)S(1)} %get-tuple-element.39, f32[1024,1024]{0,1:T(8,128)S(1)} %get-tuple-element.51), kind=kOutput, calls=%fused_computation.113 | convolution fusion | flops 126877696 | bytes 8470528 | tf_op jit(solution)/shard_map/dot_general | solution.py:95
  155.6 3.5 %fusion.84 = f32[10,1024]{1,0:T(8,128)S(1)} fusion(f32[10,1024]{1,0:T(8,128)S(1)} %divide_clamp_fusion.2, f32[1024,1024]{0,1:T(8,128)S(1)} %get-tuple-element.19), kind=kOutput, calls=%fused_computation.136 | convolution fusion | flops 125829120 | bytes 4276224 | tf_op jit(solution)/shard_map/dot_general | solution.py:102
  174.6 3.9 %fusion.68 = (f32[1024]{0:T(1024)S(1)}, f32[1024,1024]{0,1:T(8,128)S(1)}, f32[1024,1024]{0,1:T(8,128)S(1)}) fusion(f32[1024,1024]{0,1:T(8,128)S(1)} %get-tuple-element.38, f32[10,1024]{1,0:T(8,128)S(1)} %get-tuple-element.8, f32[10,1024]{1,0:T(8,128)S(1)} %get-tuple-element.15), kind=kOutput, calls=%fused_computation.125 | convolution fusion | flops 128973824 | bytes 12668928 | tf_op jit(solution)/shard_map/dot_general | solution.py:78
  178.5 3.5 %fusion.53 = f32[10,1024]{1,0:T(8,128)S(1)} fusion(f32[10,1024]{1,0:T(8,128)S(1)} %get-tuple-element.8, f32[1024,1024]{0,1:T(8,128)S(1)} %get-tuple-element.39, f32[1024,1024]{0,1:T(8,128)S(1)} %get-tuple-element.52), kind=kOutput, calls=%fused_computation.110 | convolution fusion | flops 126877696 | bytes 8470528 | tf_op jit(solution)/shard_map/dot_general | solution.py:95
  182.0 3.5 %fusion.85 = f32[10,1024]{1,0:T(8,128)S(1)} fusion(f32[10,1024]{1,0:T(8,128)S(1)} %get-tuple-element.8, f32[1024,1024]{0,1:T(8,128)S(1)} %get-tuple-element.12), kind=kOutput, calls=%fused_computation.137 | convolution fusion | flops 125829120 | bytes 4276224 | tf_op jit(solution)/shard_map/dot_general | solution.py:102
  228.3 3.9 %fusion.66 = (f32[1024]{0:T(1024)S(1)}, f32[1024,1024]{0,1:T(8,128)S(1)}, f32[1024,1024]{0,1:T(8,128)S(1)}) fusion(f32[1024,1024]{0,1:T(8,128)S(1)} %get-tuple-element.38, f32[10,1024]{1,0:T(8,128)S(1)} %add_clamp_fusion, f32[10,1024]{1,0:T(8,128)S(1)} %get-tuple-element.5, f32[1024]{0:T(1024)S(1)} %get-tuple-element.4), kind=kOutput, calls=%fused_computation.123 | convolution fusion | flops 128984064 | bytes 12673024 | tf_op jit(solution)/shard_map/dot_general | solution.py:78
  232.3 3.6 %fusion.49 = f32[10,1024]{1,0:T(8,128)S(1)} fusion(f32[10,1024]{1,0:T(8,128)S(1)} %get-tuple-element.5, f32[1024]{0:T(1024)S(1)} %get-tuple-element.4, f32[1024,1024]{0,1:T(8,128)S(1)} %get-tuple-element.39, f32[1024,1024]{0,1:T(8,128)S(1)} %get-tuple-element.53), kind=kOutput, calls=%fused_computation.106 | convolution fusion | flops 126887936 | bytes 8474624 | tf_op jit(solution)/shard_map/dot_general | solution.py:95
  235.9 3.5 %fusion.48 = f32[10,1024]{1,0:T(8,128)S(1)} fusion(f32[1024,1024]{0,1:T(8,128)S(1)} %get-tuple-element.3, f32[10,1024]{1,0:T(8,128)S(1)} %get-tuple-element.5, f32[1024]{0:T(1024)S(1)} %get-tuple-element.4), kind=kOutput, calls=%fused_computation.105 | convolution fusion | flops 125839360 | bytes 4280320 | tf_op jit(solution)/shard_map/dot_general | solution.py:102
  (175 shorter events, 141.5 us)
Async XLA Ops:
  12.0 18.2 %all-to-all-start = ((f32[10,4,2,128]{3,2,0,1:T(2,128)}), f32[10,4,2,128]{3,2,0,1:T(2,128)S(1)}, u32[]{:S(2)}, u32[]{:S(2)}) async-start(f32[10,4,2,128]{3,2,0,1:T(2,128)} %copy.14), calls=%async_computation | async-start | bytes 81920 | tf_op jit(solution)/shard_map/all_to_all | solution.py:67
  51.4 5.9 %collective-permute-start.1 = (f32[11,1024]{1,0:T(8,128)S(1)}, f32[11,1024]{1,0:T(8,128)S(1)}, u32[]{:S(2)}, u32[]{:S(2)}) collective-permute-start(f32[11,1024]{1,0:T(8,128)S(1)} %pad_maximum_fusion.6), channel_id=1, source_target_pairs={{0,2},{1,3},{2,0},{3,1},{4,6},{5,7},{6,4},{7,5},{8,10},{9,11},{10,... | collective-permute-start | bytes 135176 | tf_op jit(solution)/shard_map/ppermute | solution.py:47
  54.4 6.2 %collective-permute-start.2 = (f32[11,1024]{1,0:T(8,128)S(1)}, f32[11,1024]{1,0:T(8,128)S(1)}, u32[]{:S(2)}, u32[]{:S(2)}) collective-permute-start(f32[11,1024]{1,0:T(8,128)S(1)} %pad_maximum_fusion.6), channel_id=1, source_target_pairs={{0,3},{1,2},{2,1},{3,0},{4,7},{5,6},{6,5},{7,4},{8,11},{9,10},{10,... | collective-permute-start | bytes 135176 | tf_op jit(solution)/shard_map/ppermute | solution.py:47
  83.1 6.8 %collective-permute-start.9 = (f32[10,1024]{1,0:T(8,128)S(1)}, f32[10,1024]{1,0:T(8,128)S(1)}, u32[]{:S(2)}, u32[]{:S(2)}) collective-permute-start(f32[10,1024]{1,0:T(8,128)S(1)} %fusion.18), channel_id=1, source_target_pairs={{0,3},{1,2},{2,1},{3,0},{4,7},{5,6},{6,5},{7,4},{8,11},{9,10},{10,... | collective-permute-start | bytes 122888 | tf_op jit(solution)/shard_map/ppermute | solution.py:47
  87.5 14.7 %collective-permute-start.14 = (f32[20,1024]{1,0:T(8,128)S(1)}, f32[20,1024]{1,0:T(8,128)S(1)}, u32[]{:S(2)}, u32[]{:S(2)}) collective-permute-start(f32[20,1024]{1,0:T(8,128)S(1)} %pad_maximum_fusion.1), channel_id=1, source_target_pairs={{0,4},{4,0},{8,12},{12,8},{16,20},{20,16},{24,28},{28,24},{1,5},{5... | collective-permute-start | bytes 245768 | tf_op jit(solution)/shard_map/ppermute | solution.py:47
  133.2 7.3 %collective-permute-start.24 = (f32[20,1024]{1,0:T(8,128)S(1)}, f32[20,1024]{1,0:T(8,128)S(1)}, u32[]{:S(2)}, u32[]{:S(2)}) collective-permute-start(f32[20,1024]{1,0:T(8,128)S(1)} %pad_maximum_fusion.2), channel_id=1, source_target_pairs={{0,4},{4,0},{8,12},{12,8},{16,20},{20,16},{24,28},{28,24},{1,5},{5... | collective-permute-start | bytes 245768 | tf_op jit(solution)/shard_map/ppermute | solution.py:47
  136.0 6.8 %collective-permute-start.23 = (f32[10,1024]{1,0:T(8,128)S(1)}, f32[10,1024]{1,0:T(8,128)S(1)}, u32[]{:S(2)}, u32[]{:S(2)}) collective-permute-start(f32[10,1024]{1,0:T(8,128)S(1)} %fusion.21), channel_id=1, source_target_pairs={{0,3},{1,2},{2,1},{3,0},{4,7},{5,6},{6,5},{7,4},{8,11},{9,10},{10,... | collective-permute-start | bytes 122888 | tf_op jit(solution)/shard_map/ppermute | solution.py:47
  138.0 7.1 %collective-permute-start.22 = (f32[10,1024]{1,0:T(8,128)S(1)}, f32[10,1024]{1,0:T(8,128)S(1)}, u32[]{:S(2)}, u32[]{:S(2)}) collective-permute-start(f32[10,1024]{1,0:T(8,128)S(1)} %fusion.21), channel_id=1, source_target_pairs={{0,2},{1,3},{2,0},{3,1},{4,6},{5,7},{6,4},{7,5},{8,10},{9,11},{10,... | collective-permute-start | bytes 122888 | tf_op jit(solution)/shard_map/ppermute | solution.py:47
  138.0 7.1 %collective-permute-start.21 = (f32[10,1024]{1,0:T(8,128)S(1)}, f32[10,1024]{1,0:T(8,128)S(1)}, u32[]{:S(2)}, u32[]{:S(2)}) collective-permute-start(f32[10,1024]{1,0:T(8,128)S(1)} %fusion.21), channel_id=1, source_target_pairs={{0,1},{1,0},{2,3},{3,2},{4,5},{5,4},{6,7},{7,6},{8,9},{9,8},{10,11... | collective-permute-start | bytes 122888 | tf_op jit(solution)/shard_map/ppermute | solution.py:47
  140.4 6.5 %collective-permute-start.27 = (f32[20,1024]{1,0:T(8,128)S(1)}, f32[20,1024]{1,0:T(8,128)S(1)}, u32[]{:S(2)}, u32[]{:S(2)}) collective-permute-start(f32[20,1024]{1,0:T(8,128)S(1)} %fusion.120), channel_id=1, source_target_pairs={{0,24},{4,28},{8,16},{12,20},{16,8},{20,12},{24,0},{28,4},{1,25},{... | collective-permute-start | bytes 245768 | tf_op jit(solution)/shard_map/ppermute | solution.py:47
  159.2 7.3 %collective-permute-start.31 = (f32[20,1024]{1,0:T(8,128)S(1)}, f32[20,1024]{1,0:T(8,128)S(1)}, u32[]{:S(2)}, u32[]{:S(2)}) collective-permute-start(f32[20,1024]{1,0:T(8,128)S(1)} %pad_maximum_fusion.3), channel_id=1, source_target_pairs={{0,4},{4,0},{8,12},{12,8},{16,20},{20,16},{24,28},{28,24},{1,5},{5... | collective-permute-start | bytes 245768 | tf_op jit(solution)/shard_map/ppermute | solution.py:47
  162.0 6.8 %collective-permute-start.30 = (f32[10,1024]{1,0:T(8,128)S(1)}, f32[10,1024]{1,0:T(8,128)S(1)}, u32[]{:S(2)}, u32[]{:S(2)}) collective-permute-start(f32[10,1024]{1,0:T(8,128)S(1)} %fusion.24), channel_id=1, source_target_pairs={{0,3},{1,2},{2,1},{3,0},{4,7},{5,6},{6,5},{7,4},{8,11},{9,10},{10,... | collective-permute-start | bytes 122888 | tf_op jit(solution)/shard_map/ppermute | solution.py:47
  164.1 7.1 %collective-permute-start.29 = (f32[10,1024]{1,0:T(8,128)S(1)}, f32[10,1024]{1,0:T(8,128)S(1)}, u32[]{:S(2)}, u32[]{:S(2)}) collective-permute-start(f32[10,1024]{1,0:T(8,128)S(1)} %fusion.24), channel_id=1, source_target_pairs={{0,2},{1,3},{2,0},{3,1},{4,6},{5,7},{6,4},{7,5},{8,10},{9,11},{10,... | collective-permute-start | bytes 122888 | tf_op jit(solution)/shard_map/ppermute | solution.py:47
  164.1 7.1 %collective-permute-start.28 = (f32[10,1024]{1,0:T(8,128)S(1)}, f32[10,1024]{1,0:T(8,128)S(1)}, u32[]{:S(2)}, u32[]{:S(2)}) collective-permute-start(f32[10,1024]{1,0:T(8,128)S(1)} %fusion.24), channel_id=1, source_target_pairs={{0,1},{1,0},{2,3},{3,2},{4,5},{5,4},{6,7},{7,6},{8,9},{9,8},{10,11... | collective-permute-start | bytes 122888 | tf_op jit(solution)/shard_map/ppermute | solution.py:47
  166.5 6.5 %collective-permute-start.34 = (f32[20,1024]{1,0:T(8,128)S(1)}, f32[20,1024]{1,0:T(8,128)S(1)}, u32[]{:S(2)}, u32[]{:S(2)}) collective-permute-start(f32[20,1024]{1,0:T(8,128)S(1)} %fusion.119), channel_id=1, source_target_pairs={{0,24},{4,28},{8,16},{12,20},{16,8},{20,12},{24,0},{28,4},{1,25},{... | collective-permute-start | bytes 245768 | tf_op jit(solution)/shard_map/ppermute | solution.py:47
  188.4 6.4 %collective-permute-start.37 = (f32[10,1024]{1,0:T(8,128)S(1)}, f32[10,1024]{1,0:T(8,128)S(1)}, u32[]{:S(2)}, u32[]{:S(2)}) collective-permute-start(f32[10,1024]{1,0:T(8,128)S(1)} %fusion.27), channel_id=1, source_target_pairs={{0,3},{1,2},{2,1},{3,0},{4,7},{5,6},{6,5},{7,4},{8,11},{9,10},{10,... | collective-permute-start | bytes 122888 | tf_op jit(solution)/shard_map/ppermute | solution.py:47
  190.6 6.2 %collective-permute-start.36 = (f32[10,1024]{1,0:T(8,128)S(1)}, f32[10,1024]{1,0:T(8,128)S(1)}, u32[]{:S(2)}, u32[]{:S(2)}) collective-permute-start(f32[10,1024]{1,0:T(8,128)S(1)} %fusion.27), channel_id=1, source_target_pairs={{0,2},{1,3},{2,0},{3,1},{4,6},{5,7},{6,4},{7,5},{8,10},{9,11},{10,... | collective-permute-start | bytes 122888 | tf_op jit(solution)/shard_map/ppermute | solution.py:47
  190.6 6.2 %collective-permute-start.35 = (f32[10,1024]{1,0:T(8,128)S(1)}, f32[10,1024]{1,0:T(8,128)S(1)}, u32[]{:S(2)}, u32[]{:S(2)}) collective-permute-start(f32[10,1024]{1,0:T(8,128)S(1)} %fusion.27), channel_id=1, source_target_pairs={{0,1},{1,0},{2,3},{3,2},{4,5},{5,4},{6,7},{7,6},{8,9},{9,8},{10,11... | collective-permute-start | bytes 122888 | tf_op jit(solution)/shard_map/ppermute | solution.py:47
  192.9 16.3 %collective-permute-start.42 = (f32[20,1024]{1,0:T(8,128)S(1)}, f32[20,1024]{1,0:T(8,128)S(1)}, u32[]{:S(2)}, u32[]{:S(2)}) collective-permute-start(f32[20,1024]{1,0:T(8,128)S(1)} %pad_maximum_fusion.4), channel_id=1, source_target_pairs={{0,4},{4,0},{8,12},{12,8},{16,20},{20,16},{24,28},{28,24},{1,5},{5... | collective-permute-start | bytes 245768 | tf_op jit(solution)/shard_map/ppermute | solution.py:47
  239.5 7.3 %collective-permute-start.52 = (f32[20,1024]{1,0:T(8,128)S(1)}, f32[20,1024]{1,0:T(8,128)S(1)}, u32[]{:S(2)}, u32[]{:S(2)}) collective-permute-start(f32[20,1024]{1,0:T(8,128)S(1)} %pad_maximum_fusion.5), channel_id=1, source_target_pairs={{0,4},{4,0},{8,12},{12,8},{16,20},{20,16},{24,28},{28,24},{1,5},{5... | collective-permute-start | bytes 245768 | tf_op jit(solution)/shard_map/ppermute | solution.py:47
  242.4 6.8 %collective-permute-start.51 = (f32[10,1024]{1,0:T(8,128)S(1)}, f32[10,1024]{1,0:T(8,128)S(1)}, u32[]{:S(2)}, u32[]{:S(2)}) collective-permute-start(f32[10,1024]{1,0:T(8,128)S(1)} %fusion.30), channel_id=1, source_target_pairs={{0,3},{1,2},{2,1},{3,0},{4,7},{5,6},{6,5},{7,4},{8,11},{9,10},{10,... | collective-permute-start | bytes 122888 | tf_op jit(solution)/shard_map/ppermute | solution.py:47
  244.4 7.1 %collective-permute-start.50 = (f32[10,1024]{1,0:T(8,128)S(1)}, f32[10,1024]{1,0:T(8,128)S(1)}, u32[]{:S(2)}, u32[]{:S(2)}) collective-permute-start(f32[10,1024]{1,0:T(8,128)S(1)} %fusion.30), channel_id=1, source_target_pairs={{0,2},{1,3},{2,0},{3,1},{4,6},{5,7},{6,4},{7,5},{8,10},{9,11},{10,... | collective-permute-start | bytes 122888 | tf_op jit(solution)/shard_map/ppermute | solution.py:47
  244.5 7.0 %collective-permute-start.49 = (f32[10,1024]{1,0:T(8,128)S(1)}, f32[10,1024]{1,0:T(8,128)S(1)}, u32[]{:S(2)}, u32[]{:S(2)}) collective-permute-start(f32[10,1024]{1,0:T(8,128)S(1)} %fusion.30), channel_id=1, source_target_pairs={{0,1},{1,0},{2,3},{3,2},{4,5},{5,4},{6,7},{7,6},{8,9},{9,8},{10,11... | collective-permute-start | bytes 122888 | tf_op jit(solution)/shard_map/ppermute | solution.py:47
  246.8 6.5 %collective-permute-start.55 = (f32[20,1024]{1,0:T(8,128)S(1)}, f32[20,1024]{1,0:T(8,128)S(1)}, u32[]{:S(2)}, u32[]{:S(2)}) collective-permute-start(f32[20,1024]{1,0:T(8,128)S(1)} %fusion.116), channel_id=1, source_target_pairs={{0,24},{4,28},{8,16},{12,20},{16,8},{20,12},{24,0},{28,4},{1,25},{... | collective-permute-start | bytes 245768 | tf_op jit(solution)/shard_map/ppermute | solution.py:47
  (34 other events, 158.9 us)
